TPU v7x, 256 devices: a whole 4x4x8 slice. The times are simulated.
256 devices in a mesh: coord: 32 (over y, z), cohort: 8 (over x, core).
Axes of the slice: x: 4, y: 4, z: 8, core: 2. Of those that a mesh axis runs over, the one named last changes fastest.
Arguments:
- shapes: bfloat16 [8, 1024, 131072], P('cohort', None, 'coord'), may hold values from -6 to 6
- sketch_signs: int32 [8, 1024, 128], P('cohort'), may hold values from -1 to 1
- merge_sketch: float32 [2, 2, 128, 128], replicated, may hold values from -1.5 to 1.5
Outputs:
- basis: float32 [8, 131072, 128], P('cohort', 'coord')
- scores: float32 [8, 1024, 128], P('cohort', 'coord')
All inputs are finite; a program needn't handle non-finite values.
Results may differ from a plain program's by a relative error of at most 0.0086.
Values sent between devices are 32-bit elements; how exact they have to be, the bound alone decides.
No kernel may reach another device: no remote copies, remote signals or barrier semaphores. Data moves between devices by JAX's collectives and lax.ppermute only.
A program may use at most 64 MiB of HBM per device.

v0:
```python
import functools
import math

import jax
import jax.numpy as jnp
from jax import lax
from jax.experimental import pallas as pl
from jax.experimental.pallas import tpu as pltpu
from jax.sharding import PartitionSpec as P

HIGHEST = lax.Precision.HIGHEST
NN = (((1,), (0,)), ((), ()))
NT = (((1,), (1,)), ((), ()))
TN = (((0,), (0,)), ((), ()))
VMEM = pl.BlockSpec(memory_space=pltpu.VMEM)
SMEM = pl.BlockSpec(memory_space=pltpu.SMEM)
BLOCK = 512
WIDE = 1024


def exact(a, b, dims):
    return lax.dot_general(a, b, dims, precision=HIGHEST, preferred_element_type=jnp.float32)


def product(a, b, dims):
    return lax.dot_general(a, b, dims, preferred_element_type=jnp.float32)


def halves(x):
    high = x.astype(jnp.bfloat16)
    return high, (x - high.astype(jnp.float32)).astype(jnp.bfloat16)


def vmem(mebibytes):
    return pltpu.CompilerParams(vmem_limit_bytes=mebibytes << 20)


def cost(flops, bytes_accessed):
    return pl.CostEstimate(flops=flops, bytes_accessed=bytes_accessed, transcendentals=0)


def struct(*shape):
    return jax.ShapeDtypeStruct(shape, jnp.float32)


def sketch_kernel(half_ref, shapes_ref, signs_ref, mean_ref, sketch_ref, turned_ref):
    @pl.when(pl.program_id(0) == 0)
    def _():
        turned_ref[...] = signs_ref[...].astype(jnp.float32).T.astype(jnp.bfloat16)

    data = shapes_ref[...].astype(jnp.float32)
    mean = jnp.sum(data, axis=0, keepdims=True) * (1.0 / data.shape[0])
    mean_ref[...] = mean
    centered = (data - mean).astype(jnp.bfloat16)
    sketch_ref[...] = product(turned_ref[...], centered, NN)


def sketched(half, shapes, signs):
    subjects, coords = shapes.shape
    steps = coords // 2 // BLOCK
    return pl.pallas_call(
        sketch_kernel,
        grid_spec=pltpu.PrefetchScalarGridSpec(
            num_scalar_prefetch=1,
            grid=(steps,),
            in_specs=[
                pl.BlockSpec((subjects, BLOCK), lambda i, half: (0, half[0] * steps + i)),
                pl.BlockSpec((subjects, 128), lambda i, half: (0, 0)),
            ],
            out_specs=[
                pl.BlockSpec((1, BLOCK), lambda i, half: (0, i)),
                pl.BlockSpec((128, BLOCK), lambda i, half: (0, i)),
            ],
            scratch_shapes=[pltpu.VMEM((128, subjects), jnp.bfloat16)],
        ),
        out_shape=[struct(1, coords // 2), struct(128, coords // 2)],
        cost_estimate=cost(1 << 30, 5 << 20),
        compiler_params=vmem(48),
        name="sketch",
    )(half, shapes, signs)


def cross_kernel(pairs, *refs):
    out_ref = refs[-1]
    total = None
    for p in range(pairs):
        first, second, other = refs[3 * p : 3 * p + 3]
        for start in range(0, first.shape[1], 1024):
            cut = pl.ds(start, 1024)
            high, low = halves(jnp.concatenate([first[:, cut], second[:, cut]], axis=0))
            other_high, other_low = halves(other[:, cut])
            both = product(high, jnp.concatenate([other_high, other_low], axis=0), NT)
            part = both[:, :128] + both[:, 128:] + product(low, other_high, NT)
            total = part if total is None else total + part
    out_ref[...] = total


def cross_grams(*groups):
    return pl.pallas_call(
        functools.partial(cross_kernel, len(groups)),
        in_specs=[VMEM] * (3 * len(groups)),
        out_specs=VMEM,
        out_shape=struct(256, 128),
        cost_estimate=cost(1 << 30, 4 << 20),
        compiler_params=vmem(12),
        name="cross_grams",
    )(*[array for group in groups for array in group])


def subject_kernel(started, half_ref, shapes_ref, mean_ref, first_ref, second_ref, *refs):
    out_ref = refs[-1]
    peers, lines, _ = out_ref.shape
    lines //= 2
    centered = (shapes_ref[...].astype(jnp.float32) - mean_ref[...]).astype(jnp.bfloat16)
    first, second = halves(first_ref[...]), halves(second_ref[...])
    sums = product(centered, jnp.concatenate([first[0], second[0]], axis=0), NT)
    sums = sums + product(centered, jnp.concatenate([first[1], second[1]], axis=0), NT)
    parts = [sums[:, 128 * k : 128 * k + 128].reshape(peers, lines, 128) for k in range(2)]

    @pl.when(pl.program_id(0) == 0)
    def _():
        for k, part in enumerate(parts):
            rows = slice(lines * k, lines * k + lines)
            out_ref[:, rows, :] = part + refs[0][:, rows, :] if started else part

    @pl.when(pl.program_id(0) > 0)
    def _():
        for k, part in enumerate(parts):
            out_ref[:, lines * k : lines * k + lines, :] += part


def subject_sums(peers, half, shapes, mean, first, second, start=None):
    subjects, coords = shapes.shape
    steps = coords // 2 // WIDE
    rows = pl.BlockSpec((128, WIDE), lambda i, half: (0, i))
    shape = (peers, 2 * subjects // peers, 128)
    whole = pl.BlockSpec(shape, lambda i, half: (0, 0, 0))
    given = [] if start is None else [start]
    return pl.pallas_call(
        functools.partial(subject_kernel, bool(given)),
        grid_spec=pltpu.PrefetchScalarGridSpec(
            num_scalar_prefetch=1,
            grid=(steps,),
            in_specs=[
                pl.BlockSpec((subjects, WIDE), lambda i, half: (0, half[0] * steps + i)),
                pl.BlockSpec((1, WIDE), lambda i, half: (0, i)),
                rows,
                rows,
            ]
            + [whole] * len(given),
            out_specs=whole,
        ),
        out_shape=struct(*shape),
        cost_estimate=cost(4 << 30, 6 << 20),
        compiler_params=vmem(44),
        name="subject_sums",
    )(half, shapes, mean, first, second, *given)


def wide(line):
    return jnp.broadcast_to(line, (8, 128))


def factor_inverse(matrix):
    count = matrix.shape[0] // 8
    tiles = [matrix[8 * i : 8 * i + 8, :] for i in range(count)]
    lane = lax.broadcasted_iota(jnp.int32, (8, 128), 1)
    sub = lax.broadcasted_iota(jnp.int32, (8, 128), 0)
    inverse = [(lane == sub + 8 * i).astype(jnp.float32) for i in range(count)]
    done = []
    for p in range(count):
        rows, ident_rows = tiles[p], inverse[p]
        cols = [wide(rows[:, 8 * p + t : 8 * p + t + 1]) for t in range(8)]
        d = [[wide(cols[t][s : s + 1, :]) if s >= t else None for t in range(8)] for s in range(8)]
        low = [[None] * 8 for _ in range(8)]
        inv = [[None] * 8 for _ in range(8)]
        for s in range(8):
            root = lax.rsqrt(d[s][s])
            for t in range(s + 1, 8):
                low[t][s] = d[t][s] * root
            for t in range(s + 1, 8):
                for u in range(s + 1, t + 1):
                    d[t][u] = d[t][u] - low[t][s] * low[u][s]
            inv[s][s] = root
            for c in range(s):
                acc = low[s][c] * inv[c][c]
                for u in range(c + 1, s):
                    acc = acc + low[s][u] * inv[u][c]
                inv[s][c] = -root * acc

        def solved(block):
            lines = [wide(block[s : s + 1, :]) for s in range(8)]
            return [sum(inv[t][s] * lines[s] for s in range(t + 1)) for t in range(8)]

        def solved_twice(lines):
            return [sum(inv[t][s] * lines[t] for t in range(7, s - 1, -1)) for s in range(8)]

        final = solved(ident_rows)
        tile = final[7]
        for t in range(7):
            tile = jnp.where(sub == t, final[t], tile)
        done.append(tile)
        if p == count - 1:
            break
        left, right = solved_twice(solved(rows)), solved_twice(final)
        for i in range(p + 1, count):
            c = [wide(tiles[i][:, 8 * p + s : 8 * p + s + 1]) for s in range(8)]
            tiles[i] = tiles[i] - sum(c[s] * left[s] for s in range(8))
            inverse[i] = inverse[i] - sum(c[s] * right[s] for s in range(8))
    return jnp.concatenate(done, axis=0)


def merged_gram(maps_ref, cross):
    lower, upper = maps_ref[0, 0], maps_ref[0, 1]
    return exact(lower, lower, TN) + exact(upper, upper, TN) + cross + cross.T


def part_of(shape, *index):
    return pl.BlockSpec(shape, lambda i: index)


def level_maps(level):
    return part_of((1, 2, 128, 128), level, 0, 0, 0)


def own_level_kernel(side_ref, gram_ref, maps_ref, out_ref):
    inverse = factor_inverse(gram_ref[...].reshape(128, 128))
    out_ref[...] = exact(inverse, maps_ref[0, side_ref[0]], TN)


def own_level(side, pair, maps):
    return pl.pallas_call(
        own_level_kernel,
        grid=(1,),
        in_specs=[SMEM, part_of((16, 8, 128), 0, 0, 0), level_maps(0)],
        out_specs=VMEM,
        out_shape=struct(128, 128),
        cost_estimate=cost(7 << 30, 1 << 20),
        compiler_params=vmem(4),
        name="own_level",
    )(side, pair, maps)


def pair_level_kernel(own_ref, mate_ref, cross_ref, maps_ref, out_ref):
    own, mate = own_ref[...], mate_ref[...]
    cross = exact(mate, exact(cross_ref[...].reshape(128, 128), own, NN), TN)
    inverse = factor_inverse(merged_gram(maps_ref, cross))
    out_ref[0:128, :] = exact(own, inverse, NT)
    out_ref[128:256, :] = exact(mate, inverse, NT)


def pair_level(own, mate, pair, maps):
    return pl.pallas_call(
        pair_level_kernel,
        grid=(1,),
        in_specs=[VMEM, VMEM, part_of((16, 8, 128), 1, 0, 0), level_maps(0)],
        out_specs=VMEM,
        out_shape=struct(256, 128),
        cost_estimate=cost(8 << 30, 1 << 20),
        compiler_params=vmem(4),
        name="pair_level",
    )(own, mate, pair, maps)


def far_cross_kernel(side_ref, near_ref, cross_ref, far_ref, out_ref):
    cross = exact(near_ref[...], cross_ref[...].reshape(256, 128), TN)
    cross = exact(cross, far_ref[0:128, :], NN)
    out_ref[...] = jnp.where(side_ref[0] == 1, cross.T, cross)


def far_cross_term(side, near, cross, far):
    return pl.pallas_call(
        far_cross_kernel,
        grid=(1,),
        in_specs=[SMEM, VMEM, part_of((32, 8, 128), 0, 0, 0), VMEM],
        out_specs=VMEM,
        out_shape=struct(128, 128),
        cost_estimate=cost(1 << 29, 1 << 20),
        compiler_params=vmem(4),
        name="far_cross",
    )(side, near, cross, far)


def mixed(a, b, dims):
    (a_high, a_low), (b_high, b_low) = halves(a), halves(b)
    return product(a_high, b_high, dims) + (
        product(a_high, b_low, dims) + product(a_low, b_high, dims)
    )


def far_terms_kernel(sums_ref, far_ref, out_ref):
    peers, lines, _ = out_ref.shape
    total = None
    for k in range(2):
        sums = sums_ref[:, lines * k : lines * k + lines, :].reshape(peers * lines, 128)
        part = mixed(sums, far_ref[128 * k : 128 * k + 128, :], NN)
        total = part if total is None else total + part
    out_ref[...] = total.reshape(out_ref.shape)


def far_terms(sums, far):
    peers, lines, width = sums.shape
    return pl.pallas_call(
        far_terms_kernel,
        in_specs=[VMEM] * 2,
        out_specs=VMEM,
        out_shape=struct(peers, lines // 2, width),
        cost_estimate=cost(1 << 29, 2 << 20),
        compiler_params=vmem(10),
        name="far_terms",
    )(sums, far)


def last_level_kernel(scale, side_ref, cross_ref, maps_ref, near_ref, far_ref, *refs):
    sources, (basis_ref, own_ref, other_ref, held, done, sems, out_sems) = refs[:8], refs[8:]
    side = side_ref[0]
    half = held.shape[2]
    loads = [
        pltpu.make_async_copy(
            source, held.at[k // 4, pl.ds(k % 4 * 128, 128), :], sems.at[k]
        )
        for k, source in enumerate(sources)
    ]
    for load in loads:
        load.start()
    lower, upper = maps_ref[0, 0], maps_ref[0, 1]
    cross = exact(exact(lower, cross_ref[...], TN), upper, NN)
    inverse = factor_inverse(merged_gram(maps_ref, cross))
    own = exact(maps_ref[0, side], inverse, NT)
    other = exact(maps_ref[0, 1 - side], inverse, NT)
    near = exact(near_ref[...], own, NN)
    own_ref[...] = near
    other_ref[...] = other
    maps = jnp.concatenate([near, exact(far_ref[...], other, NN)], axis=0).T * scale
    maps_high, maps_low = halves(maps)
    both_maps = jnp.concatenate([maps_high, maps_low], axis=0)
    stores = []
    for slot, start in ((0, side * half), (1, (1 - side) * half)):
        for load in loads[4 * slot : 4 * slot + 4]:
            load.wait()
        for chunk in range(half // BLOCK):
            high, low = halves(held[slot, :, chunk * BLOCK : chunk * BLOCK + BLOCK])
            both = product(both_maps, high, NN)
            rows = (both[:128] + both[128:] + product(maps_high, low, NN)).T
            k = slot * (half // BLOCK) + chunk
            done[k] = rows
            store = pltpu.make_async_copy(
                done.at[k], basis_ref.at[pl.ds(start + chunk * BLOCK, BLOCK), :], out_sems.at[k]
            )
            store.start()
            stores.append(store)
    for store in stores:
        store.wait()


def last_level(side, cross, maps, near, far, kept, given, scale):
    half = kept[0].shape[1]
    chunks = 2 * half // BLOCK
    return pl.pallas_call(
        functools.partial(last_level_kernel, scale),
        grid=(1,),
        in_specs=[SMEM, VMEM, level_maps(1), VMEM, VMEM]
        + [pl.BlockSpec(memory_space=pl.ANY)] * 8,
        out_specs=[pl.BlockSpec(memory_space=pl.ANY), VMEM, VMEM],
        out_shape=[struct(2 * half, 128), struct(256, 128), struct(128, 128)],
        scratch_shapes=[
            pltpu.VMEM((2, 512, half), jnp.float32),
            pltpu.VMEM((chunks, BLOCK, 128), jnp.float32),
            pltpu.SemaphoreType.DMA((8,)),
            pltpu.SemaphoreType.DMA((chunks,)),
        ],
        cost_estimate=cost(12 << 30, 10 << 20),
        compiler_params=vmem(50),
        name="last_level",
    )(side, cross, maps, near, far, *kept, *given)


def scores_kernel(scale, near_ref, far_ref, own_ref, other_ref, out_ref):
    lines = out_ref.shape[0]
    total = mixed(jnp.sum(far_ref[...], axis=0), other_ref[...], NN)
    for k in range(2):
        rows = near_ref[lines * k : lines * k + lines, :]
        total = total + mixed(rows, own_ref[128 * k : 128 * k + 128, :], NN)
    out_ref[...] = total * scale


def scores_of(near, far, own, other, scale):
    return pl.pallas_call(
        functools.partial(scores_kernel, scale),
        in_specs=[VMEM] * 4,
        out_specs=VMEM,
        out_shape=struct(near.shape[0] // 2, 128),
        cost_estimate=cost(1 << 29, 1 << 20),
        compiler_params=vmem(4),
        name="scores",
    )(near, far, own, other)


def to_each(lines, axis):
    count = lax.axis_size(axis)
    return lines.reshape(count, -1, lines.shape[-1])


def to_all(part, axis):
    return jnp.broadcast_to(part[None], (lax.axis_size(axis), *part.shape))


def exchanged(blocks, axis):
    return lax.all_to_all(blocks, axis, 0, 0, tiled=True)


def across(shard, bit):
    return lax.ppermute(shard, "cohort", [(i, i ^ bit) for i in range(lax.axis_size("cohort"))])


def after(value, *others):
    return lax.optimization_barrier((value, *others))[0]


def on_device(shapes, sketch_signs, merge_sketch):
    shapes, signs = shapes[0], sketch_signs[0]
    peers = lax.axis_size("coord")
    position = lax.axis_index("cohort")
    side = (position & 1).reshape(1)
    upper = (position >> 1 & 1).reshape(1)

    mean_given, own_given = sketched(1 - upper, shapes, signs)
    far_kept = across(own_given, 2)
    mean_kept, own_kept = sketched(upper, shapes, signs)
    mate_given = across(own_given, 1)
    mate_kept = across(own_kept, 1)
    pair = cross_grams((own_given, mate_given, own_given), (own_kept, mate_kept, own_kept))
    later = after(shapes, pair)
    pair = exchanged(to_each(pair, "coord"), "coord")
    near_sums = subject_sums(peers, 1 - upper, later, mean_given, own_given, mate_given)
    near_sums = subject_sums(peers, upper, later, mean_kept, own_kept, mate_kept, near_sums)
    pair_part = jnp.sum(pair, axis=0)
    lines = pair_part.shape[0]
    far_kept = after(far_kept, near_sums, pair_part)

    far_cross = cross_grams((own_kept, mate_kept, far_kept))
    far_given = across(after(own_kept, far_kept), 2)
    far_mate_kept = across(far_kept, 1)
    both = exchanged(
        jnp.concatenate([to_all(pair_part, "coord"), to_each(far_cross, "coord")], axis=1), "coord"
    )
    far_sums = subject_sums(peers, upper, shapes, mean_kept, far_kept, far_mate_kept)
    both = after(both, far_sums)
    far_part = jnp.sum(both[:, lines:], axis=0)
    far_cross = exchanged(
        jnp.concatenate([to_all(far_part, "coord"), near_sums], axis=1), "coord"
    )

    own_map = own_level(side, both, merge_sketch)
    mate_map = across(own_map, 1)
    near = pair_level(own_map, mate_map, both, merge_sketch)
    far = across(near, 2)
    far_given = after(far_given, own_map)
    far_mate_given = across(far_given, 1)
    far_sums = subject_sums(
        peers, 1 - upper, after(shapes, near), mean_given, far_given, far_mate_given, far_sums
    )

    far = after(far, far_sums)
    near_sums = jnp.sum(far_cross[:, lines:], axis=0)
    far_cross = far_cross_term(upper, near, far_cross, far)
    far_cross = far_cross + across(far_cross, 1)
    far_sums = exchanged(far_terms(far_sums, after(far, far_cross)), "coord")
    far_cross = far_cross + across(far_cross, 2)

    total = shapes.shape[1] * peers
    basis, own_map, other_map = last_level(
        upper,
        far_cross,
        merge_sketch,
        near,
        far,
        (own_kept, mate_kept, far_kept, far_mate_kept),
        (own_given, mate_given, far_given, far_mate_given),
        math.sqrt(total),
    )
    factor = 4.0 * math.sqrt(basis.shape[1] / total)
    scores = scores_of(near_sums, far_sums, own_map, other_map, factor)
    return basis[None], scores[None]


def solution(mesh):
    placed = (P("cohort", None, "coord"), P("cohort", None, None), P())
    return jax.shard_map(
        on_device,
        mesh=mesh,
        in_specs=placed,
        out_specs=(P("cohort", "coord", None), P("cohort", "coord", None)),
        check_vma=False,
    )
```

profile of v0, /device:TPU:34, one launch (start us, length us, event | category | flops | bytes accessed | tf_op | source)
XLA Modules:
  0.0 129.1 jit_solution(11043155984840376477)
XLA Ops:
  0.6 0.0 copy-start.1
  0.6 1.0 copy-done.1
  1.7 4.7 %sketch.2 = (f32[1,2048]{1,0:T(1,128)S(1)}, f32[128,2048]{1,0:T(8,128)S(1)}) custom-call(s32[1]{0:T(128)S(6)} %sub.2.half_ref, bf16[1024,4096]{1,0:T(8,128)(2,1)} %bitcast.11, s32[1024,128]{1,0:T(8,128)S(1)} %bitcast.8), custom_call_target="tpu_custom_call" | custom-call | flops 1073741824 | bytes 5242880 | tf_op jit(solution)/shard_map/sketch/pallas_call | solution.py:61
  6.4 0.0 copy-start
  6.4 0.1 collective-permute-start
  6.5 0.0 copy-done.2
  6.5 4.9 %sketch.3 = (f32[1,2048]{1,0:T(1,128)S(1)}, f32[128,2048]{1,0:T(8,128)S(1)}) custom-call(s32[1]{0:T(128)} %bitcast.half_ref.side_ref, bf16[1024,4096]{1,0:T(8,128)(2,1)} %bitcast.12, s32[1024,128]{1,0:T(8,128)S(1)} %bitcast.9), custom_call_target="tpu_custom_call" | custom-call | flops 1073741824 | bytes 5242880 | tf_op jit(solution)/shard_map/sketch/pallas_call | solution.py:61
  11.4 0.3 collective-permute-start.1
  11.7 0.5 collective-permute-start.2
  12.2 0.0 collective-permute-done.refs_1_.second_ref.refs_5_
  12.2 1.9 %collective-permute-done.1.refs_4_.second_ref.refs_1_ = f32[128,2048]{1,0:T(8,128)S(1)} collective-permute-done((f32[128,2048]{1,0:T(8,128)S(1)}, f32[128,2048]{1,0:T(8,128)S(1)}, u32[]{:S(2)}, u32[]{:S(2)}) %collective-permute-start.1) | collective-permute-done | bytes 1048608 | tf_op jit(solution)/shard_map/ppermute | solution.py:413
  14.1 1.9 %cross_grams.2 = f32[256,128]{1,0:T(8,128)} custom-call(f32[128,2048]{1,0:T(8,128)S(1)} %get-tuple-element.17.refs_0_.refs_2_.first_ref.refs_4_, f32[128,2048]{1,0:T(8,128)S(1)} %collective-permute-done.refs_1_.second_ref.refs_5_, f32[128,2048]{1,0:T(8,128)S(1)} %get-tuple-element.17.refs_0_.refs_2_.first_ref.refs_4_, ...), custom_call_target="tpu_custom_call" | custom-call | flops 1073741824 | bytes 4194304 | tf_op jit(solution)/shard_map/cross_grams/pallas_call | solution.py:99
  16.0 0.0 copy-done.4
  16.0 11.4 %all-to-all-start = ((f32[32,8,128]{2,1,0:T(8,128)}), f32[32,8,128]{2,1,0:T(8,128)S(1)}, u32[]{:S(2)}, u32[]{:S(2)}) async-start(f32[32,8,128]{2,1,0:T(8,128)} %bitcast.4), calls=%async_computation | async-start | bytes 262144 | tf_op jit(solution)/shard_map/all_to_all | solution.py:409
  27.4 0.0 copy-done
  27.4 0.0 copy-done.3
  27.4 0.0 copy-start.5
  27.4 4.5 %subject_sums.4.refs_0_ = f32[32,64,128]{2,1,0:T(8,128)S(1)} custom-call(s32[1]{0:T(128)S(6)} %sub.2.half_ref, bf16[1024,4096]{1,0:T(8,128)(2,1)} %bitcast.13, f32[1,2048]{1,0:T(1,128)S(1)} %get-tuple-element.21.mean_ref, f32[128,2048]{1,0:T(8,128)S(1)} %get-tuple-element.17.refs_0_.refs_2_.first_ref.refs_4_, ...), custom_call_target="tpu_custom_call" | custom-call | flops 4294967296 | bytes 6291456 | tf_op jit(solution)/shard_map/subject_sums/pallas_call | solution.py:139
  31.9 0.0 copy-done.5
  31.9 0.0 copy-start.6
  31.9 4.6 %subject_sums.5 = f32[32,64,128]{2,1,0:T(8,128)S(1)} custom-call(s32[1]{0:T(128)} %bitcast.half_ref.side_ref, bf16[1024,4096]{1,0:T(8,128)(2,1)} %bitcast.14, f32[1,2048]{1,0:T(1,128)S(1)} %get-tuple-element.20.mean_ref, f32[128,2048]{1,0:T(8,128)S(1)} %get-tuple-element.25.refs_3_.refs_5_.first_ref.refs_0_, f32[128,2048]{1,0:T(8,128)S(1)} %copy-done.5, ...), custom_call_target="tpu_custom_call" | custom-call | flops 4294967296 | bytes 6291456 | tf_op jit(solution)/shard_map/subject_sums/pallas_call | solution.py:139
  36.5 0.0 copy-start.8
  36.5 1.0 copy-done.8
  37.5 0.0 all-to-all-done
  37.5 0.0 collective-permute-done.2.refs_2_.first_ref
  37.5 0.1 collective-permute-start.3
  37.6 0.0 copy-done.6
  37.6 1.9 %cross_grams.3 = f32[256,128]{1,0:T(8,128)S(1)} custom-call(f32[128,2048]{1,0:T(8,128)S(1)} %get-tuple-element.25.refs_3_.refs_5_.first_ref.refs_0_, f32[128,2048]{1,0:T(8,128)S(1)} %copy-done.6, f32[128,2048]{1,0:T(8,128)} %collective-permute-done.2.refs_2_.first_ref), custom_call_target="tpu_custom_call" | custom-call | flops 1073741824 | bytes 4194304 | tf_op jit(solution)/shard_map/cross_grams/pallas_call | solution.py:99
  39.6 0.7 pad_maximum_fusion.1
  40.3 10.8 %all-to-all-start.1 = ((f32[32,16,128]{2,1,0:T(8,128)}), f32[32,16,128]{2,1,0:T(8,128)S(1)}, u32[]{:S(2)}, u32[]{:S(2)}) async-start(f32[32,16,128]{2,1,0:T(8,128)} %pad_maximum_fusion.1), calls=%async_computation.1 | async-start | bytes 524288 | tf_op jit(solution)/shard_map/all_to_all | solution.py:409
  51.2 0.0 copy-start.9
  51.2 0.6 collective-permute-start.6
  51.8 0.0 collective-permute-done.3.second_ref.refs_3_
  51.8 4.7 %subject_sums.6.refs_0_ = f32[32,64,128]{2,1,0:T(8,128)S(1)} custom-call(s32[1]{0:T(128)} %bitcast.half_ref.side_ref, bf16[1024,4096]{1,0:T(8,128)(2,1)} %bitcast.15, f32[1,2048]{1,0:T(1,128)S(1)} %get-tuple-element.20.mean_ref, f32[128,2048]{1,0:T(8,128)} %collective-permute-done.2.refs_2_.first_ref, f32[128,2048]{1,0:T(8,128)} %collective-permute-done.3.second_ref.refs_3_), custom_call_target="tpu_custom_call" | custom-call | flops 4294967296 | bytes 6291456 | tf_op jit(solution)/shard_map/subject_sums/pallas_call | solution.py:139
  56.5 1.0 copy-done.14
  57.5 6.6 %all-to-all-done.1.gram_ref.cross_ref = f32[32,16,128]{2,1,0:T(8,128)S(1)} async-done(((f32[32,16,128]{2,1,0:T(8,128)}), f32[32,16,128]{2,1,0:T(8,128)S(1)}, u32[]{:S(2)}, u32[]{:S(2)}) %all-to-all-start.1) | async-done | bytes 262176 | tf_op jit(solution)/shard_map/all_to_all | solution.py:409
  64.2 1.1 pad_maximum_fusion
  65.3 4.7 %all-to-all-start.2 = ((f32[32,72,128]{2,1,0:T(8,128)}), f32[32,72,128]{2,1,0:T(8,128)S(1)}, u32[]{:S(2)}, u32[]{:S(2)}) async-start(f32[32,72,128]{2,1,0:T(8,128)} %pad_maximum_fusion), calls=%async_computation.2 | async-start | bytes 2359296 | tf_op jit(solution)/shard_map/all_to_all | solution.py:409
  70.0 5.1 %own_level.1.own_ref = f32[128,128]{1,0:T(8,128)S(1)} custom-call(s32[1]{0:T(128)} %bitcast.1.side_ref, f32[32,16,128]{2,1,0:T(8,128)S(1)} %all-to-all-done.1.gram_ref.cross_ref, f32[2,2,128,128]{3,2,1,0:T(8,128)S(1)} %copy-done.11), custom_call_target="tpu_custom_call" | custom-call | flops 7516192768 | bytes 1048576 | tf_op jit(solution)/shard_map/own_level/pallas_call | solution.py:232
  75.2 1.2 collective-permute-done.6.first_ref.refs_6_
  76.4 0.0 collective-permute-start.7
  76.4 0.5 collective-permute-start.4
  76.9 1.9 %collective-permute-done.4.mate_ref = f32[128,128]{1,0:T(8,128)S(1)} collective-permute-done((f32[128,128]{1,0:T(8,128)S(1)}, f32[128,128]{1,0:T(8,128)S(1)}, u32[]{:S(2)}, u32[]{:S(2)}) %collective-permute-start.4) | collective-permute-done | bytes 65568 | tf_op jit(solution)/shard_map/ppermute | solution.py:413
  78.8 6.2 %pair_level.1.near_ref = f32[256,128]{1,0:T(8,128)S(1)} custom-call(f32[128,128]{1,0:T(8,128)S(1)} %own_level.1.own_ref, f32[128,128]{1,0:T(8,128)S(1)} %collective-permute-done.4.mate_ref, f32[32,16,128]{2,1,0:T(8,128)S(1)} %all-to-all-done.1.gram_ref.cross_ref, f32[2,2,128,128]{3,2,1,0:T(8,128)S(1)} %copy-done.11), custom_call_target="tpu_custom_call" | custom-call | flops 8589934592 | bytes 1048576 | tf_op jit(solution)/shard_map/pair_level/pallas_call | solution.py:253
  85.0 0.6 collective-permute-start.5
  85.6 0.0 collective-permute-done.7.second_ref.refs_7_
  85.6 5.0 %subject_sums.7.sums_ref = f32[32,64,128]{2,1,0:T(8,128)S(1)} custom-call(s32[1]{0:T(128)S(6)} %sub.2.half_ref, bf16[1024,4096]{1,0:T(8,128)(2,1)} %bitcast.16, f32[1,2048]{1,0:T(1,128)S(1)} %get-tuple-element.21.mean_ref, f32[128,2048]{1,0:T(8,128)} %collective-permute-done.6.first_ref.refs_6_, f32[128,2048]{1,0:T(8,128)S(1)} %collective-permute-done.7.second_ref.refs_7_, ...), custom_call_target="tpu_custom_call" | custom-call | flops 4294967296 | bytes 6291456 | tf_op jit(solution)/shard_map/subject_sums/pallas_call | solution.py:139
  90.6 0.0 copy-done.10
  90.6 0.0 copy-start.12
  90.6 1.1 copy-done.12
  91.7 0.0 collective-permute-done.5.far_ref
  91.7 9.3 %all-to-all-done.2.cross_ref = f32[32,72,128]{2,1,0:T(8,128)S(1)} async-done(((f32[32,72,128]{2,1,0:T(8,128)}), f32[32,72,128]{2,1,0:T(8,128)S(1)}, u32[]{:S(2)}, u32[]{:S(2)}) %all-to-all-start.2) | async-done | bytes 1179680 | tf_op jit(solution)/shard_map/all_to_all | solution.py:409
  101.0 0.6 far_cross.1
  101.6 0.3 collective-permute-start.8
  102.0 1.2 collective-permute-done.8
  103.2 0.6 collective-permute-start.9
  103.8 0.1 slice_reduce_fusion.near_ref
  103.9 1.4 %far_terms.1 = f32[32,32,128]{2,1,0:T(8,128)} custom-call(f32[32,64,128]{2,1,0:T(8,128)S(1)} %copy-done.13, f32[256,128]{1,0:T(8,128)S(1)} %collective-permute-done.5.far_ref), custom_call_target="tpu_custom_call" | custom-call | flops 536870912 | bytes 2097152 | tf_op jit(solution)/shard_map/far_terms/pallas_call | solution.py:303
  105.3 5.3 %all-to-all-start.3 = ((f32[32,32,128]{2,1,0:T(8,128)}), f32[32,32,128]{2,1,0:T(8,128)S(1)}, u32[]{:S(2)}, u32[]{:S(2)}) async-start(f32[32,32,128]{2,1,0:T(8,128)} %far_terms.1), calls=%async_computation.3 | async-start | bytes 1048576 | tf_op jit(solution)/shard_map/all_to_all | solution.py:409
  110.6 0.0 collective-permute-done.9
  110.7 0.0 copy-done.7
  110.7 11.5 %last_level.1 = (f32[4096,128]{1,0:T(8,128)}, f32[256,128]{1,0:T(8,128)S(1)}, f32[128,128]{1,0:T(8,128)S(1)}) custom-call(s32[1]{0:T(128)} %bitcast.half_ref.side_ref, f32[128,128]{1,0:T(8,128)S(1)} %add.7.cross_ref, f32[2,2,128,128]{3,2,1,0:T(8,128)S(1)} %copy-done.11, f32[256,128]{1,0:T(8,128)S(1)} %pair_level.1.near_ref, ...), custom_call_target="tpu_custom_call" | custom-call | flops 12884901888 | bytes 10485760 | tf_op jit(solution)/shard_map/last_level/pallas_call | solution.py:359
  122.2 6.1 %all-to-all-done.3.far_ref = f32[32,32,128]{2,1,0:T(8,128)S(1)} async-done(((f32[32,32,128]{2,1,0:T(8,128)}), f32[32,32,128]{2,1,0:T(8,128)S(1)}, u32[]{:S(2)}, u32[]{:S(2)}) %all-to-all-start.3) | async-done | bytes 524320 | tf_op jit(solution)/shard_map/all_to_all | solution.py:409
  128.3 0.8 scores.1
  (19 shorter events, 0.1 us)
Async XLA Ops:
  0.6 1.0 copy-start.1
  1.7 4.8 %copy-start.2 = (s32[1,1024,128]{2,1,0:T(8,128)S(1)}, s32[1,1024,128]{2,1,0:T(8,128)}, u32[]{:S(2)}) copy-start(s32[1,1024,128]{2,1,0:T(8,128)} %param.4) | copy-start | bytes 1572868
  6.4 21.0 %copy-start = (f32[128,2048]{1,0:T(8,128)}, f32[128,2048]{1,0:T(8,128)S(1)}, u32[]{:S(2)}) copy-start(f32[128,2048]{1,0:T(8,128)S(1)} %get-tuple-element.17.refs_0_.refs_2_.first_ref.refs_4_) | copy-start | bytes 3145732
  6.4 5.8 %collective-permute-start = (f32[128,2048]{1,0:T(8,128)S(1)}, f32[128,2048]{1,0:T(8,128)S(1)}, u32[]{:S(2)}, u32[]{:S(2)}) collective-permute-start(f32[128,2048]{1,0:T(8,128)S(1)} %get-tuple-element.17.refs_0_.refs_2_.first_ref.refs_4_), channel_id=1, source_target_pairs={{0,1},{1,0},{2,3},{3,2},{4,5},{5,4},{6,7},{7,6},{8,9},{9,8},{10,11... | collective-permute-start | bytes 3145736 | tf_op jit(solution)/shard_map/ppermute | solution.py:413
  11.4 2.7 %collective-permute-start.1 = (f32[128,2048]{1,0:T(8,128)S(1)}, f32[128,2048]{1,0:T(8,128)S(1)}, u32[]{:S(2)}, u32[]{:S(2)}) collective-permute-start(f32[128,2048]{1,0:T(8,128)S(1)} %get-tuple-element.25.refs_3_.refs_5_.first_ref.refs_0_), channel_id=1, source_target_pairs={{0,1},{1,0},{2,3},{3,2},{4,5},{5,4},{6,7},{7,6},{8,9},{9,8},{10,11... | collective-permute-start | bytes 3145736 | tf_op jit(solution)/shard_map/ppermute | solution.py:413
  11.7 25.9 %collective-permute-start.2 = (f32[128,2048]{1,0:T(8,128)S(1)}, f32[128,2048]{1,0:T(8,128)}, u32[]{:S(2)}, u32[]{:S(2)}) collective-permute-start(f32[128,2048]{1,0:T(8,128)S(1)} %get-tuple-element.17.refs_0_.refs_2_.first_ref.refs_4_), channel_id=1, source_target_pairs={{0,2},{1,3},{2,0},{3,1},{4,6},{5,7},{6,4},{7,5},{8,10},{9,11},{10,... | collective-permute-start | bytes 3145736 | tf_op jit(solution)/shard_map/ppermute | solution.py:413
  12.2 15.2 %copy-start.3 = (f32[128,2048]{1,0:T(8,128)}, f32[128,2048]{1,0:T(8,128)S(1)}, u32[]{:S(2)}) copy-start(f32[128,2048]{1,0:T(8,128)S(1)} %collective-permute-done.refs_1_.second_ref.refs_5_) | copy-start | bytes 3145732
  14.1 1.9 %copy-start.4 = (f32[128,2048]{1,0:T(8,128)}, f32[128,2048]{1,0:T(8,128)S(1)}, u32[]{:S(2)}) copy-start(f32[128,2048]{1,0:T(8,128)S(1)} %collective-permute-done.1.refs_4_.second_ref.refs_1_) | copy-start | bytes 3145732
  16.0 21.5 %all-to-all-start = ((f32[32,8,128]{2,1,0:T(8,128)}), f32[32,8,128]{2,1,0:T(8,128)S(1)}, u32[]{:S(2)}, u32[]{:S(2)}) async-start(f32[32,8,128]{2,1,0:T(8,128)} %bitcast.4), calls=%async_computation | async-start | bytes 262144 | tf_op jit(solution)/shard_map/all_to_all | solution.py:409
  27.4 4.5 %copy-start.5 = (f32[128,2048]{1,0:T(8,128)S(1)}, f32[128,2048]{1,0:T(8,128)}, u32[]{:S(2)}) copy-start(f32[128,2048]{1,0:T(8,128)} %copy-done.4) | copy-start | bytes 3145732
  31.9 5.7 %copy-start.6 = (f32[128,2048]{1,0:T(8,128)S(1)}, f32[128,2048]{1,0:T(8,128)}, u32[]{:S(2)}) copy-start(f32[128,2048]{1,0:T(8,128)} %copy-done.4) | copy-start | bytes 3145732
  36.5 1.0 copy-start.8
  37.5 14.3 %collective-permute-start.3 = (f32[128,2048]{1,0:T(8,128)}, f32[128,2048]{1,0:T(8,128)}, u32[]{:S(2)}, u32[]{:S(2)}) collective-permute-start(f32[128,2048]{1,0:T(8,128)} %collective-permute-done.2.refs_2_.first_ref), channel_id=1, source_target_pairs={{0,1},{1,0},{2,3},{3,2},{4,5},{5,4},{6,7},{7,6},{8,9},{9,8},{10,11... | collective-permute-start | bytes 3145736 | tf_op jit(solution)/shard_map/ppermute | solution.py:413
  40.3 23.8 %all-to-all-start.1 = ((f32[32,16,128]{2,1,0:T(8,128)}), f32[32,16,128]{2,1,0:T(8,128)S(1)}, u32[]{:S(2)}, u32[]{:S(2)}) async-start(f32[32,16,128]{2,1,0:T(8,128)} %pad_maximum_fusion.1), calls=%async_computation.1 | async-start | bytes 524288 | tf_op jit(solution)/shard_map/all_to_all | solution.py:409
  51.2 13.0 %copy-start.9 = (f32[32,64,128]{2,1,0:T(8,128)S(1)}, f32[32,64,128]{2,1,0:T(8,128)}, u32[]{:S(2)}) copy-start(f32[32,64,128]{2,1,0:T(8,128)} %copy-done.8) | copy-start | bytes 3145732
  51.2 25.2 %collective-permute-start.6 = (f32[128,2048]{1,0:T(8,128)S(1)}, f32[128,2048]{1,0:T(8,128)}, u32[]{:S(2)}, u32[]{:S(2)}) collective-permute-start(f32[128,2048]{1,0:T(8,128)S(1)} %get-tuple-element.25.refs_3_.refs_5_.first_ref.refs_0_), channel_id=1, source_target_pairs={{0,2},{1,3},{2,0},{3,1},{4,6},{5,7},{6,4},{7,5},{8,10},{9,11},{10,... | collective-permute-start | bytes 3145736 | tf_op jit(solution)/shard_map/ppermute | solution.py:413
  56.5 1.0 copy-start.14
  65.3 4.8 %copy-start.11 = (f32[2,2,128,128]{3,2,1,0:T(8,128)S(1)}, f32[2,2,128,128]{3,2,1,0:T(8,128)}, u32[]{:S(2)}) copy-start(f32[2,2,128,128]{3,2,1,0:T(8,128)} %maps_ref.5) | copy-start | bytes 786436
  65.3 35.7 %all-to-all-start.2 = ((f32[32,72,128]{2,1,0:T(8,128)}), f32[32,72,128]{2,1,0:T(8,128)S(1)}, u32[]{:S(2)}, u32[]{:S(2)}) async-start(f32[32,72,128]{2,1,0:T(8,128)} %pad_maximum_fusion), calls=%async_computation.2 | async-start | bytes 2359296 | tf_op jit(solution)/shard_map/all_to_all | solution.py:409
  75.2 10.4 %copy-start.15 = (f32[32,64,128]{2,1,0:T(8,128)S(1)}, f32[32,64,128]{2,1,0:T(8,128)}, u32[]{:S(2)}) copy-start(f32[32,64,128]{2,1,0:T(8,128)} %copy-done.14) | copy-start | bytes 3145732
  76.4 9.2 %collective-permute-start.7 = (f32[128,2048]{1,0:T(8,128)}, f32[128,2048]{1,0:T(8,128)S(1)}, u32[]{:S(2)}, u32[]{:S(2)}) collective-permute-start(f32[128,2048]{1,0:T(8,128)} %collective-permute-done.6.first_ref.refs_6_), channel_id=1, source_target_pairs={{0,1},{1,0},{2,3},{3,2},{4,5},{5,4},{6,7},{7,6},{8,9},{9,8},{10,11... | collective-permute-start | bytes 3145736 | tf_op jit(solution)/shard_map/ppermute | solution.py:413
  76.4 2.4 %collective-permute-start.4 = (f32[128,128]{1,0:T(8,128)S(1)}, f32[128,128]{1,0:T(8,128)S(1)}, u32[]{:S(2)}, u32[]{:S(2)}) collective-permute-start(f32[128,128]{1,0:T(8,128)S(1)} %own_level.1.own_ref), channel_id=1, source_target_pairs={{0,1},{1,0},{2,3},{3,2},{4,5},{5,4},{6,7},{7,6},{8,9},{9,8},{10,11... | collective-permute-start | bytes 196616 | tf_op jit(solution)/shard_map/ppermute | solution.py:413
  85.0 6.7 %collective-permute-start.5 = (f32[256,128]{1,0:T(8,128)S(1)}, f32[256,128]{1,0:T(8,128)S(1)}, u32[]{:S(2)}, u32[]{:S(2)}) collective-permute-start(f32[256,128]{1,0:T(8,128)S(1)} %pair_level.1.near_ref), channel_id=1, source_target_pairs={{0,2},{1,3},{2,0},{3,1},{4,6},{5,7},{6,4},{7,5},{8,10},{9,11},{10,... | collective-permute-start | bytes 393224 | tf_op jit(solution)/shard_map/ppermute | solution.py:413
  85.6 5.0 %copy-start.10 = (f32[128,2048]{1,0:T(8,128)}, f32[128,2048]{1,0:T(8,128)S(1)}, u32[]{:S(2)}) copy-start(f32[128,2048]{1,0:T(8,128)S(1)} %collective-permute-done.7.second_ref.refs_7_) | copy-start | bytes 3145732
  90.6 1.1 copy-start.12
  101.0 2.9 %copy-start.13 = (f32[32,64,128]{2,1,0:T(8,128)S(1)}, f32[32,64,128]{2,1,0:T(8,128)}, u32[]{:S(2)}) copy-start(f32[32,64,128]{2,1,0:T(8,128)} %copy-done.12) | copy-start | bytes 3145732
  101.6 1.6 %collective-permute-start.8 = (f32[128,128]{1,0:T(8,128)S(1)}, f32[128,128]{1,0:T(8,128)S(1)}, u32[]{:S(2)}, u32[]{:S(2)}) collective-permute-start(f32[128,128]{1,0:T(8,128)S(1)} %far_cross.1), channel_id=1, source_target_pairs={{0,1},{1,0},{2,3},{3,2},{4,5},{5,4},{6,7},{7,6},{8,9},{9,8},{10,11... | collective-permute-start | bytes 196616 | tf_op jit(solution)/shard_map/ppermute | solution.py:413
  103.2 7.4 %collective-permute-start.9 = (f32[128,128]{1,0:T(8,128)S(1)}, f32[128,128]{1,0:T(8,128)S(1)}, u32[]{:S(2)}, u32[]{:S(2)}) collective-permute-start(f32[128,128]{1,0:T(8,128)S(1)} %add.6), channel_id=1, source_target_pairs={{0,2},{1,3},{2,0},{3,1},{4,6},{5,7},{6,4},{7,5},{8,10},{9,11},{10,... | collective-permute-start | bytes 196616 | tf_op jit(solution)/shard_map/ppermute | solution.py:413
  103.9 6.8 %copy-start.7 = (f32[128,2048]{1,0:T(8,128)S(1)}, f32[128,2048]{1,0:T(8,128)}, u32[]{:S(2)}) copy-start(f32[128,2048]{1,0:T(8,128)} %copy-done.4) | copy-start | bytes 3145732
  105.3 23.0 %all-to-all-start.3 = ((f32[32,32,128]{2,1,0:T(8,128)}), f32[32,32,128]{2,1,0:T(8,128)S(1)}, u32[]{:S(2)}, u32[]{:S(2)}) async-start(f32[32,32,128]{2,1,0:T(8,128)} %far_terms.1), calls=%async_computation.3 | async-start | bytes 1048576 | tf_op jit(solution)/shard_map/all_to_all | solution.py:409
where the time goes:
time: 131 us; the launch traced here: 129 us
  Pallas kernels  57.7 us (44%)
  starting transfers between devices  36 us (27%)
  waiting for transfers between devices  28.3 us (22%)
  local copies, waits for them, and re-layouts  4.11 us (3%)
  other arithmetic  1.98 us (2%)
    all_to_all x4, starting transfers between devices, exchanged(): return lax.all_to_all(blocks, axis, 0, 0, tiled=True)  32.3 us
    all_to_all x4, waiting for transfers between devices, exchanged(): return lax.all_to_all(blocks, axis, 0, 0, tiled=True)  22.1 us
    pallas_call x4, Pallas kernels, subject_sums(): pl.pallas_call(functools.partial(subject_kernel, bool(given)), grid_spec=...  18.7 us
    pallas_call x1, Pallas kernels, last_level(): pl.pallas_call(functools.partial(last_level_kernel, scale), grid=(1,), in...  11.5 us
    pallas_call x2, Pallas kernels, sketched(): pl.pallas_call(sketch_kernel, grid_spec=pltpu.PrefetchScalarGridSpec(num_...  9.53 us
    ppermute x10, waiting for transfers between devices, across(): lax.ppermute(shard, 'cohort', [(i, i ^ bit) for i in range(lax.axis_size(...  6.24 us
    pallas_call x1, Pallas kernels, pair_level(): pl.pallas_call(pair_level_kernel, grid=(1,), in_specs=[VMEM, VMEM, part_o...  6.17 us
    pallas_call x1, Pallas kernels, own_level(): pl.pallas_call(own_level_kernel, grid=(1,), in_specs=[SMEM, part_of((16,...  5.14 us
  transfers between devices with their start and end apart: 14, of which 7 were waited for; matrix products, arithmetic and copies ran while one was open for 2% of the time, Pallas kernels for 40%

commit v1 on v0

--- a/solution.py
+++ b/solution.py
@@ -288,27 +288,28 @@
     )
 
 
-def far_terms_kernel(sums_ref, far_ref, out_ref):
+def far_terms_kernel(kept_ref, given_ref, far_ref, out_ref):
     peers, lines, _ = out_ref.shape
     total = None
     for k in range(2):
-        sums = sums_ref[:, lines * k : lines * k + lines, :].reshape(peers * lines, 128)
+        rows = slice(lines * k, lines * k + lines)
+        sums = (kept_ref[:, rows, :] + given_ref[:, rows, :]).reshape(peers * lines, 128)
         part = mixed(sums, far_ref[128 * k : 128 * k + 128, :], NN)
         total = part if total is None else total + part
     out_ref[...] = total.reshape(out_ref.shape)
 
 
-def far_terms(sums, far):
-    peers, lines, width = sums.shape
+def far_terms(kept, given, far):
+    peers, lines, width = kept.shape
     return pl.pallas_call(
         far_terms_kernel,
-        in_specs=[VMEM] * 2,
+        in_specs=[VMEM] * 3,
         out_specs=VMEM,
         out_shape=struct(peers, lines // 2, width),
         cost_estimate=cost(1 << 29, 2 << 20),
         compiler_params=vmem(10),
         name="far_terms",
-    )(sums, far)
+    )(kept, given, far)
 
 
 def last_level_kernel(scale, side_ref, cross_ref, maps_ref, near_ref, far_ref, *refs):
@@ -444,28 +445,30 @@
     both = exchanged(
         jnp.concatenate([to_all(pair_part, "coord"), to_each(far_cross, "coord")], axis=1), "coord"
     )
-    far_sums = subject_sums(peers, upper, shapes, mean_kept, far_kept, far_mate_kept)
-    both = after(both, far_sums)
+    far_sums_kept = subject_sums(peers, upper, shapes, mean_kept, far_kept, far_mate_kept)
+    near_sums = jnp.pad(near_sums, ((0, 0), (lines, 0), (0, 0)))
+    both, near_sums, _ = lax.optimization_barrier((both, near_sums, far_sums_kept))
     far_part = jnp.sum(both[:, lines:], axis=0)
     far_cross = exchanged(
-        jnp.concatenate([to_all(far_part, "coord"), near_sums], axis=1), "coord"
+        lax.dynamic_update_slice(near_sums, to_all(far_part, "coord"), (0, 0, 0)), "coord"
     )
 
     own_map = own_level(side, both, merge_sketch)
     mate_map = across(own_map, 1)
     near = pair_level(own_map, mate_map, both, merge_sketch)
     far = across(near, 2)
-    far_given = after(far_given, own_map)
+    far_given = after(far_given, mate_map)
     far_mate_given = across(far_given, 1)
     far_sums = subject_sums(
-        peers, 1 - upper, after(shapes, near), mean_given, far_given, far_mate_given, far_sums
-    )
-
+        peers, 1 - upper, after(shapes, near), mean_given, far_given, far_mate_given
+    )
+
+    far_sums = far_terms(far_sums_kept, far_sums, far)
     far = after(far, far_sums)
     near_sums = jnp.sum(far_cross[:, lines:], axis=0)
     far_cross = far_cross_term(upper, near, far_cross, far)
     far_cross = far_cross + across(far_cross, 1)
-    far_sums = exchanged(far_terms(far_sums, after(far, far_cross)), "coord")
+    far_sums = exchanged(after(far_sums, far_cross), "coord")
     far_cross = far_cross + across(far_cross, 2)
 
     total = shapes.shape[1] * peers

time: 131 us -> 129 us (0.985); the launches traced: 129 us -> 129 us
  waiting for transfers between devices: 28.3 us -> 21.5 us
  local copies, waits for them, and re-layouts: 4.11 us -> 8.81 us
  starting transfers between devices: 36 us -> 38 us
    all_to_all x4, waiting for transfers between devices: 22.1 us -> 17.1 us  [exchanged(): return lax.all_to_all(blocks, axis, 0, 0, tiled=True)]
    unnamed x32 -> x36, local copies, waits for them, and re-layouts: 4.09 us -> 7.03 us
    ppermute x10, waiting for transfers between devices: 6.24 us -> 4.39 us  [across(): lax.ppermute(shard, 'cohort', [(i, i ^ bit) for i in range(lax.axis_size(...]
    ppermute x10, starting transfers between devices: 3.74 us -> 5.3 us  [across(): lax.ppermute(shard, 'cohort', [(i, i ^ bit) for i in range(lax.axis_size(...]
  transfers between devices with their start and end apart: 14 -> 14, of which waited for: 7 -> 6; matrix products, arithmetic and copies ran while one was open for 2% -> 3% of each run, Pallas kernels for 40% -> 40%
where the time goes in v1:
time: 129 us
  Pallas kernels  57.5 us (45%)
  starting transfers between devices  38 us (29%)
  waiting for transfers between devices  21.5 us (17%)
  local copies, waits for them, and re-layouts  8.81 us (7%)
  other arithmetic  1.72 us (1%)
    all_to_all x4, starting transfers between devices, exchanged(): return lax.all_to_all(blocks, axis, 0, 0, tiled=True)  32.7 us
    pallas_call x4, Pallas kernels, subject_sums(): pl.pallas_call(functools.partial(subject_kernel, bool(given)), grid_spec=...  18.4 us
    all_to_all x4, waiting for transfers between devices, exchanged(): return lax.all_to_all(blocks, axis, 0, 0, tiled=True)  17.1 us
    pallas_call x1, Pallas kernels, last_level(): pl.pallas_call(functools.partial(last_level_kernel, scale), grid=(1,), in...  11.5 us
    pallas_call x2, Pallas kernels, sketched(): pl.pallas_call(sketch_kernel, grid_spec=pltpu.PrefetchScalarGridSpec(num_...  9.53 us
    unnamed x36, local copies, waits for them, and re-layouts  7.03 us
    pallas_call x1, Pallas kernels, pair_level(): pl.pallas_call(pair_level_kernel, grid=(1,), in_specs=[VMEM, VMEM, part_o...  6.17 us
    ppermute x10, starting transfers between devices, across(): lax.ppermute(shard, 'cohort', [(i, i ^ bit) for i in range(lax.axis_size(...  5.3 us
  transfers between devices with their start and end apart: 14, of which 6 were waited for; matrix products, arithmetic and copies ran while one was open for 3% of the time, Pallas kernels for 40%

profile of v1, /device:TPU:34, one launch (start us, length us, event | category | flops | bytes accessed | tf_op | source)
XLA Modules:
  0.0 128.6 jit_solution(2930022457428228443)
XLA Ops:
  0.6 0.0 copy-start.1
  0.6 1.0 copy-done.1
  1.7 4.7 %sketch.2 = (f32[1,2048]{1,0:T(1,128)S(1)}, f32[128,2048]{1,0:T(8,128)S(1)}) custom-call(s32[1]{0:T(128)S(6)} %sub.2.half_ref, bf16[1024,4096]{1,0:T(8,128)(2,1)} %bitcast.11, s32[1024,128]{1,0:T(8,128)S(1)} %bitcast.8), custom_call_target="tpu_custom_call" | custom-call | flops 1073741824 | bytes 5242880 | tf_op jit(solution)/shard_map/sketch/pallas_call | solution.py:61
  6.4 0.1 collective-permute-start
  6.5 4.9 %sketch.3 = (f32[1,2048]{1,0:T(1,128)S(1)}, f32[128,2048]{1,0:T(8,128)S(1)}) custom-call(s32[1]{0:T(128)} %bitcast.half_ref.side_ref, bf16[1024,4096]{1,0:T(8,128)(2,1)} %bitcast.12, s32[1024,128]{1,0:T(8,128)S(1)} %bitcast.9), custom_call_target="tpu_custom_call" | custom-call | flops 1073741824 | bytes 5242880 | tf_op jit(solution)/shard_map/sketch/pallas_call | solution.py:61
  11.4 0.3 collective-permute-start.1
  11.7 0.5 collective-permute-start.2
  12.2 0.0 collective-permute-done.refs_1_.second_ref.refs_5_
  12.2 1.9 %collective-permute-done.1.refs_4_.second_ref.refs_1_ = f32[128,2048]{1,0:T(8,128)S(1)} collective-permute-done((f32[128,2048]{1,0:T(8,128)S(1)}, f32[128,2048]{1,0:T(8,128)S(1)}, u32[]{:S(2)}, u32[]{:S(2)}) %collective-permute-start.1) | collective-permute-done | bytes 1048608 | tf_op jit(solution)/shard_map/ppermute | solution.py:414
  14.1 1.9 %cross_grams.2 = f32[256,128]{1,0:T(8,128)} custom-call(f32[128,2048]{1,0:T(8,128)S(1)} %get-tuple-element.18.refs_0_.refs_2_.first_ref.refs_4_, f32[128,2048]{1,0:T(8,128)S(1)} %collective-permute-done.refs_1_.second_ref.refs_5_, f32[128,2048]{1,0:T(8,128)S(1)} %get-tuple-element.18.refs_0_.refs_2_.first_ref.refs_4_, ...), custom_call_target="tpu_custom_call" | custom-call | flops 1073741824 | bytes 4194304 | tf_op jit(solution)/shard_map/cross_grams/pallas_call | solution.py:99
  16.0 11.4 %all-to-all-start = ((f32[32,8,128]{2,1,0:T(8,128)}), f32[32,8,128]{2,1,0:T(8,128)S(1)}, u32[]{:S(2)}, u32[]{:S(2)}) async-start(f32[32,8,128]{2,1,0:T(8,128)} %bitcast.4), calls=%async_computation | async-start | bytes 262144 | tf_op jit(solution)/shard_map/all_to_all | solution.py:410
  27.4 4.5 %subject_sums.4.refs_0_ = f32[32,64,128]{2,1,0:T(8,128)S(1)} custom-call(s32[1]{0:T(128)S(6)} %sub.2.half_ref, bf16[1024,4096]{1,0:T(8,128)(2,1)} %bitcast.13, f32[1,2048]{1,0:T(1,128)S(1)} %get-tuple-element.22.mean_ref, f32[128,2048]{1,0:T(8,128)S(1)} %get-tuple-element.18.refs_0_.refs_2_.first_ref.refs_4_, ...), custom_call_target="tpu_custom_call" | custom-call | flops 4294967296 | bytes 6291456 | tf_op jit(solution)/shard_map/subject_sums/pallas_call | solution.py:139
  31.9 4.6 %subject_sums.5 = f32[32,64,128]{2,1,0:T(8,128)S(1)} custom-call(s32[1]{0:T(128)} %bitcast.half_ref.side_ref, bf16[1024,4096]{1,0:T(8,128)(2,1)} %bitcast.14, f32[1,2048]{1,0:T(1,128)S(1)} %get-tuple-element.21.mean_ref, f32[128,2048]{1,0:T(8,128)S(1)} %get-tuple-element.27.refs_3_.refs_5_.first_ref.refs_0_, f32[128,2048]{1,0:T(8,128)S(1)} %copy-done.5, ...), custom_call_target="tpu_custom_call" | custom-call | flops 4294967296 | bytes 6291456 | tf_op jit(solution)/shard_map/subject_sums/pallas_call | solution.py:139
  36.5 0.0 copy-start.8
  36.5 1.0 copy-done.8
  37.5 0.0 all-to-all-done
  37.5 0.0 collective-permute-done.2.refs_2_.first_ref
  37.5 0.1 collective-permute-start.3
  37.6 1.9 %cross_grams.3 = f32[256,128]{1,0:T(8,128)S(1)} custom-call(f32[128,2048]{1,0:T(8,128)S(1)} %get-tuple-element.27.refs_3_.refs_5_.first_ref.refs_0_, f32[128,2048]{1,0:T(8,128)S(1)} %copy-done.6, f32[128,2048]{1,0:T(8,128)} %collective-permute-done.2.refs_2_.first_ref), custom_call_target="tpu_custom_call" | custom-call | flops 1073741824 | bytes 4194304 | tf_op jit(solution)/shard_map/cross_grams/pallas_call | solution.py:99
  39.6 0.0 copy-start.9
  39.6 0.7 pad_maximum_fusion
  40.3 10.8 %all-to-all-start.1 = ((f32[32,16,128]{2,1,0:T(8,128)}), f32[32,16,128]{2,1,0:T(8,128)S(1)}, u32[]{:S(2)}, u32[]{:S(2)}) async-start(f32[32,16,128]{2,1,0:T(8,128)} %pad_maximum_fusion), calls=%async_computation.1 | async-start | bytes 524288 | tf_op jit(solution)/shard_map/all_to_all | solution.py:410
  51.2 0.0 copy-done.9
  51.2 1.1 pad.4
  52.3 0.5 collective-permute-start.6
  52.9 0.0 collective-permute-done.3.second_ref.refs_3_
  52.9 1.0 copy-done.10
  53.8 1.2 copy-done.11
  55.0 4.5 %subject_sums.6.kept_ref = f32[32,64,128]{2,1,0:T(8,128)S(1)} custom-call(s32[1]{0:T(128)} %bitcast.half_ref.side_ref, bf16[1024,4096]{1,0:T(8,128)(2,1)} %bitcast.15, f32[1,2048]{1,0:T(1,128)S(1)} %get-tuple-element.21.mean_ref, f32[128,2048]{1,0:T(8,128)} %collective-permute-done.2.refs_2_.first_ref, f32[128,2048]{1,0:T(8,128)S(1)} %copy-done.11), custom_call_target="tpu_custom_call" | custom-call | flops 4294967296 | bytes 6291456 | tf_op jit(solution)/shard_map/subject_sums/pallas_call | solution.py:139
  59.5 4.6 %all-to-all-done.1.gram_ref.cross_ref = f32[32,16,128]{2,1,0:T(8,128)S(1)} async-done(((f32[32,16,128]{2,1,0:T(8,128)}), f32[32,16,128]{2,1,0:T(8,128)S(1)}, u32[]{:S(2)}, u32[]{:S(2)}) %all-to-all-start.1) | async-done | bytes 262176 | tf_op jit(solution)/shard_map/all_to_all | solution.py:410
  64.2 0.7 broadcast_dynamic-update-slice_fusion
  64.8 5.2 %all-to-all-start.2 = ((f32[32,72,128]{2,1,0:T(8,128)}), f32[32,72,128]{2,1,0:T(8,128)S(1)}, u32[]{:S(2)}, u32[]{:S(2)}) async-start(f32[32,72,128]{2,1,0:T(8,128)} %broadcast_dynamic-update-slice_fusion), calls=%async_computation.2 | async-start | bytes 2359296 | tf_op jit(solution)/shard_map/all_to_all | solution.py:410
  70.0 0.0 copy-start.13
  70.0 0.9 copy-done.13
  71.0 5.1 %own_level.1.own_ref = f32[128,128]{1,0:T(8,128)S(1)} custom-call(s32[1]{0:T(128)} %bitcast.1.side_ref, f32[32,16,128]{2,1,0:T(8,128)S(1)} %all-to-all-done.1.gram_ref.cross_ref, f32[2,2,128,128]{3,2,1,0:T(8,128)S(1)} %copy-done.13), custom_call_target="tpu_custom_call" | custom-call | flops 7516192768 | bytes 1048576 | tf_op jit(solution)/shard_map/own_level/pallas_call | solution.py:232
  76.1 0.1 collective-permute-start.4
  76.2 1.2 collective-permute-done.6.first_ref.refs_6_
  77.4 0.0 collective-permute-done.4.mate_ref
  77.5 0.2 collective-permute-start.7
  77.6 6.2 %pair_level.1.near_ref = f32[256,128]{1,0:T(8,128)S(1)} custom-call(f32[128,128]{1,0:T(8,128)S(1)} %own_level.1.own_ref, f32[128,128]{1,0:T(8,128)S(1)} %collective-permute-done.4.mate_ref, f32[32,16,128]{2,1,0:T(8,128)S(1)} %all-to-all-done.1.gram_ref.cross_ref, f32[2,2,128,128]{3,2,1,0:T(8,128)S(1)} %copy-done.13), custom_call_target="tpu_custom_call" | custom-call | flops 8589934592 | bytes 1048576 | tf_op jit(solution)/shard_map/pair_level/pallas_call | solution.py:253
  83.8 1.8 %collective-permute-start.5 = (f32[256,128]{1,0:T(8,128)S(1)}, f32[256,128]{1,0:T(8,128)S(1)}, u32[]{:S(2)}, u32[]{:S(2)}) collective-permute-start(f32[256,128]{1,0:T(8,128)S(1)} %pair_level.1.near_ref), channel_id=1, source_target_pairs={{0,2},{1,3},{2,0},{3,1},{4,6},{5,7},{6,4},{7,5},{8,10},{9,11},{10,... | collective-permute-start | bytes 393224 | tf_op jit(solution)/shard_map/ppermute | solution.py:414
  85.6 0.0 collective-permute-done.7.second_ref.refs_7_
  85.6 4.9 %subject_sums.7.given_ref = f32[32,64,128]{2,1,0:T(8,128)S(1)} custom-call(s32[1]{0:T(128)S(6)} %sub.2.half_ref, bf16[1024,4096]{1,0:T(8,128)(2,1)} %bitcast.16, f32[1,2048]{1,0:T(1,128)S(1)} %get-tuple-element.22.mean_ref, f32[128,2048]{1,0:T(8,128)} %collective-permute-done.6.first_ref.refs_6_, f32[128,2048]{1,0:T(8,128)S(1)} %collective-permute-done.7.second_ref.refs_7_), custom_call_target="tpu_custom_call" | custom-call | flops 4294967296 | bytes 6291456 | tf_op jit(solution)/shard_map/subject_sums/pallas_call | solution.py:139
  90.5 0.0 copy-done.15
  90.5 0.0 copy-done.12
  90.5 0.0 collective-permute-done.5.far_ref
  90.6 1.4 %far_terms.1 = f32[32,32,128]{2,1,0:T(8,128)} custom-call(f32[32,64,128]{2,1,0:T(8,128)S(1)} %subject_sums.6.kept_ref, f32[32,64,128]{2,1,0:T(8,128)S(1)} %subject_sums.7.given_ref, f32[256,128]{1,0:T(8,128)S(1)} %collective-permute-done.5.far_ref), custom_call_target="tpu_custom_call" | custom-call | flops 536870912 | bytes 2097152 | tf_op jit(solution)/shard_map/far_terms/pallas_call | solution.py:304
  92.0 9.1 %all-to-all-done.2.cross_ref = f32[32,72,128]{2,1,0:T(8,128)S(1)} async-done(((f32[32,72,128]{2,1,0:T(8,128)}), f32[32,72,128]{2,1,0:T(8,128)S(1)}, u32[]{:S(2)}, u32[]{:S(2)}) %all-to-all-start.2) | async-done | bytes 1179680 | tf_op jit(solution)/shard_map/all_to_all | solution.py:410
  101.1 0.0 copy-done.16
  101.1 0.6 far_cross.1
  101.7 0.1 collective-permute-start.8
  101.8 1.2 collective-permute-done.8
  103.1 0.0 copy-start.7
  103.1 1.6 %collective-permute-start.9 = (f32[128,128]{1,0:T(8,128)S(1)}, f32[128,128]{1,0:T(8,128)}, u32[]{:S(2)}, u32[]{:S(2)}) collective-permute-start(f32[128,128]{1,0:T(8,128)S(1)} %add.8), channel_id=1, source_target_pairs={{0,2},{1,3},{2,0},{3,1},{4,6},{5,7},{6,4},{7,5},{8,10},{9,11},{10,... | collective-permute-start | bytes 196616 | tf_op jit(solution)/shard_map/ppermute | solution.py:414
  104.7 0.1 slice_reduce_fusion.near_ref
  104.7 5.3 %all-to-all-start.3 = ((f32[32,32,128]{2,1,0:T(8,128)}), f32[32,32,128]{2,1,0:T(8,128)S(1)}, u32[]{:S(2)}, u32[]{:S(2)}) async-start(f32[32,32,128]{2,1,0:T(8,128)} %far_terms.1), calls=%async_computation.3 | async-start | bytes 1048576 | tf_op jit(solution)/shard_map/all_to_all | solution.py:410
  110.1 0.0 collective-permute-done.9
  110.1 0.8 add.9.cross_ref
  110.9 0.0 copy-start.14
  110.9 0.9 copy-done.14
  111.9 0.9 copy-done.17
  112.8 11.5 %last_level.1 = (f32[4096,128]{1,0:T(8,128)}, f32[256,128]{1,0:T(8,128)S(1)}, f32[128,128]{1,0:T(8,128)S(1)}) custom-call(s32[1]{0:T(128)} %bitcast.half_ref.side_ref, f32[128,128]{1,0:T(8,128)S(1)} %add.9.cross_ref, f32[2,2,128,128]{3,2,1,0:T(8,128)S(1)} %copy-done.14, f32[256,128]{1,0:T(8,128)S(1)} %copy-done.17, ...), custom_call_target="tpu_custom_call" | custom-call | flops 12884901888 | bytes 10485760 | tf_op jit(solution)/shard_map/last_level/pallas_call | solution.py:360
  124.3 3.5 %all-to-all-done.3.far_ref = f32[32,32,128]{2,1,0:T(8,128)S(1)} async-done(((f32[32,32,128]{2,1,0:T(8,128)}), f32[32,32,128]{2,1,0:T(8,128)S(1)}, u32[]{:S(2)}, u32[]{:S(2)}) %all-to-all-start.3) | async-done | bytes 524320 | tf_op jit(solution)/shard_map/all_to_all | solution.py:410
  127.7 0.8 scores.1
  (23 shorter events, 0.1 us)
Async XLA Ops:
  0.6 1.0 copy-start.1
  1.7 4.8 %copy-start.2 = (s32[1,1024,128]{2,1,0:T(8,128)S(1)}, s32[1,1024,128]{2,1,0:T(8,128)}, u32[]{:S(2)}) copy-start(s32[1,1024,128]{2,1,0:T(8,128)} %param.4) | copy-start | bytes 1572868
  6.4 21.0 %copy-start = (f32[128,2048]{1,0:T(8,128)}, f32[128,2048]{1,0:T(8,128)S(1)}, u32[]{:S(2)}) copy-start(f32[128,2048]{1,0:T(8,128)S(1)} %get-tuple-element.18.refs_0_.refs_2_.first_ref.refs_4_) | copy-start | bytes 3145732
  6.4 5.8 %collective-permute-start = (f32[128,2048]{1,0:T(8,128)S(1)}, f32[128,2048]{1,0:T(8,128)S(1)}, u32[]{:S(2)}, u32[]{:S(2)}) collective-permute-start(f32[128,2048]{1,0:T(8,128)S(1)} %get-tuple-element.18.refs_0_.refs_2_.first_ref.refs_4_), channel_id=1, source_target_pairs={{0,1},{1,0},{2,3},{3,2},{4,5},{5,4},{6,7},{7,6},{8,9},{9,8},{10,11... | collective-permute-start | bytes 3145736 | tf_op jit(solution)/shard_map/ppermute | solution.py:414
  11.4 2.7 %collective-permute-start.1 = (f32[128,2048]{1,0:T(8,128)S(1)}, f32[128,2048]{1,0:T(8,128)S(1)}, u32[]{:S(2)}, u32[]{:S(2)}) collective-permute-start(f32[128,2048]{1,0:T(8,128)S(1)} %get-tuple-element.27.refs_3_.refs_5_.first_ref.refs_0_), channel_id=1, source_target_pairs={{0,1},{1,0},{2,3},{3,2},{4,5},{5,4},{6,7},{7,6},{8,9},{9,8},{10,11... | collective-permute-start | bytes 3145736 | tf_op jit(solution)/shard_map/ppermute | solution.py:414
  11.7 25.9 %collective-permute-start.2 = (f32[128,2048]{1,0:T(8,128)S(1)}, f32[128,2048]{1,0:T(8,128)}, u32[]{:S(2)}, u32[]{:S(2)}) collective-permute-start(f32[128,2048]{1,0:T(8,128)S(1)} %get-tuple-element.18.refs_0_.refs_2_.first_ref.refs_4_), channel_id=1, source_target_pairs={{0,2},{1,3},{2,0},{3,1},{4,6},{5,7},{6,4},{7,5},{8,10},{9,11},{10,... | collective-permute-start | bytes 3145736 | tf_op jit(solution)/shard_map/ppermute | solution.py:414
  12.2 15.2 %copy-start.3 = (f32[128,2048]{1,0:T(8,128)}, f32[128,2048]{1,0:T(8,128)S(1)}, u32[]{:S(2)}) copy-start(f32[128,2048]{1,0:T(8,128)S(1)} %collective-permute-done.refs_1_.second_ref.refs_5_) | copy-start | bytes 3145732
  14.1 1.9 %copy-start.4 = (f32[128,2048]{1,0:T(8,128)}, f32[128,2048]{1,0:T(8,128)S(1)}, u32[]{:S(2)}) copy-start(f32[128,2048]{1,0:T(8,128)S(1)} %collective-permute-done.1.refs_4_.second_ref.refs_1_) | copy-start | bytes 3145732
  16.0 21.5 %all-to-all-start = ((f32[32,8,128]{2,1,0:T(8,128)}), f32[32,8,128]{2,1,0:T(8,128)S(1)}, u32[]{:S(2)}, u32[]{:S(2)}) async-start(f32[32,8,128]{2,1,0:T(8,128)} %bitcast.4), calls=%async_computation | async-start | bytes 262144 | tf_op jit(solution)/shard_map/all_to_all | solution.py:410
  27.4 4.5 %copy-start.5 = (f32[128,2048]{1,0:T(8,128)S(1)}, f32[128,2048]{1,0:T(8,128)}, u32[]{:S(2)}) copy-start(f32[128,2048]{1,0:T(8,128)} %copy-done.4) | copy-start | bytes 3145732
  31.9 5.7 %copy-start.6 = (f32[128,2048]{1,0:T(8,128)S(1)}, f32[128,2048]{1,0:T(8,128)}, u32[]{:S(2)}) copy-start(f32[128,2048]{1,0:T(8,128)} %copy-done.4) | copy-start | bytes 3145732
  36.5 1.0 copy-start.8
  37.5 15.3 %collective-permute-start.3 = (f32[128,2048]{1,0:T(8,128)}, f32[128,2048]{1,0:T(8,128)S(1)}, u32[]{:S(2)}, u32[]{:S(2)}) collective-permute-start(f32[128,2048]{1,0:T(8,128)} %collective-permute-done.2.refs_2_.first_ref), channel_id=1, source_target_pairs={{0,1},{1,0},{2,3},{3,2},{4,5},{5,4},{6,7},{7,6},{8,9},{9,8},{10,11... | collective-permute-start | bytes 3145736 | tf_op jit(solution)/shard_map/ppermute | solution.py:414
  39.6 11.6 %copy-start.9 = (f32[32,64,128]{2,1,0:T(8,128)S(1)}, f32[32,64,128]{2,1,0:T(8,128)}, u32[]{:S(2)}) copy-start(f32[32,64,128]{2,1,0:T(8,128)} %copy-done.8) | copy-start | bytes 3145732
  40.3 23.8 %all-to-all-start.1 = ((f32[32,16,128]{2,1,0:T(8,128)}), f32[32,16,128]{2,1,0:T(8,128)S(1)}, u32[]{:S(2)}, u32[]{:S(2)}) async-start(f32[32,16,128]{2,1,0:T(8,128)} %pad_maximum_fusion), calls=%async_computation.1 | async-start | bytes 524288 | tf_op jit(solution)/shard_map/all_to_all | solution.py:410
  52.3 25.1 %collective-permute-start.6 = (f32[128,2048]{1,0:T(8,128)S(1)}, f32[128,2048]{1,0:T(8,128)}, u32[]{:S(2)}, u32[]{:S(2)}) collective-permute-start(f32[128,2048]{1,0:T(8,128)S(1)} %get-tuple-element.27.refs_3_.refs_5_.first_ref.refs_0_), channel_id=1, source_target_pairs={{0,2},{1,3},{2,0},{3,1},{4,6},{5,7},{6,4},{7,5},{8,10},{9,11},{10,... | collective-permute-start | bytes 3145736 | tf_op jit(solution)/shard_map/ppermute | solution.py:414
  52.9 1.0 copy-start.10
  53.8 1.2 copy-start.11
  64.8 36.2 %all-to-all-start.2 = ((f32[32,72,128]{2,1,0:T(8,128)}), f32[32,72,128]{2,1,0:T(8,128)S(1)}, u32[]{:S(2)}, u32[]{:S(2)}) async-start(f32[32,72,128]{2,1,0:T(8,128)} %broadcast_dynamic-update-slice_fusion), calls=%async_computation.2 | async-start | bytes 2359296 | tf_op jit(solution)/shard_map/all_to_all | solution.py:410
  70.0 1.0 copy-start.13
  76.1 1.3 %collective-permute-start.4 = (f32[128,128]{1,0:T(8,128)S(1)}, f32[128,128]{1,0:T(8,128)S(1)}, u32[]{:S(2)}, u32[]{:S(2)}) collective-permute-start(f32[128,128]{1,0:T(8,128)S(1)} %own_level.1.own_ref), channel_id=1, source_target_pairs={{0,1},{1,0},{2,3},{3,2},{4,5},{5,4},{6,7},{7,6},{8,9},{9,8},{10,11... | collective-permute-start | bytes 196616 | tf_op jit(solution)/shard_map/ppermute | solution.py:414
  77.5 8.2 %collective-permute-start.7 = (f32[128,2048]{1,0:T(8,128)}, f32[128,2048]{1,0:T(8,128)S(1)}, u32[]{:S(2)}, u32[]{:S(2)}) collective-permute-start(f32[128,2048]{1,0:T(8,128)} %collective-permute-done.6.first_ref.refs_6_), channel_id=1, source_target_pairs={{0,1},{1,0},{2,3},{3,2},{4,5},{5,4},{6,7},{7,6},{8,9},{9,8},{10,11... | collective-permute-start | bytes 3145736 | tf_op jit(solution)/shard_map/ppermute | solution.py:414
  83.8 6.7 %copy-start.15 = (f32[256,128]{1,0:T(8,128)}, f32[256,128]{1,0:T(8,128)S(1)}, u32[]{:S(2)}) copy-start(f32[256,128]{1,0:T(8,128)S(1)} %pair_level.1.near_ref) | copy-start | bytes 393220
  83.8 6.7 %collective-permute-start.5 = (f32[256,128]{1,0:T(8,128)S(1)}, f32[256,128]{1,0:T(8,128)S(1)}, u32[]{:S(2)}, u32[]{:S(2)}) collective-permute-start(f32[256,128]{1,0:T(8,128)S(1)} %pair_level.1.near_ref), channel_id=1, source_target_pairs={{0,2},{1,3},{2,0},{3,1},{4,6},{5,7},{6,4},{7,5},{8,10},{9,11},{10,... | collective-permute-start | bytes 393224 | tf_op jit(solution)/shard_map/ppermute | solution.py:414
  85.6 4.9 %copy-start.12 = (f32[128,2048]{1,0:T(8,128)}, f32[128,2048]{1,0:T(8,128)S(1)}, u32[]{:S(2)}) copy-start(f32[128,2048]{1,0:T(8,128)S(1)} %collective-permute-done.7.second_ref.refs_7_) | copy-start | bytes 3145732
  90.6 10.5 %copy-start.16 = (f32[256,128]{1,0:T(8,128)S(1)}, f32[256,128]{1,0:T(8,128)}, u32[]{:S(2)}) copy-start(f32[256,128]{1,0:T(8,128)} %copy-done.15) | copy-start | bytes 393220
  101.7 1.3 %collective-permute-start.8 = (f32[128,128]{1,0:T(8,128)S(1)}, f32[128,128]{1,0:T(8,128)S(1)}, u32[]{:S(2)}, u32[]{:S(2)}) collective-permute-start(f32[128,128]{1,0:T(8,128)S(1)} %far_cross.1), channel_id=1, source_target_pairs={{0,1},{1,0},{2,3},{3,2},{4,5},{5,4},{6,7},{7,6},{8,9},{9,8},{10,11... | collective-permute-start | bytes 196616 | tf_op jit(solution)/shard_map/ppermute | solution.py:414
  103.1 7.9 %copy-start.7 = (f32[128,2048]{1,0:T(8,128)S(1)}, f32[128,2048]{1,0:T(8,128)}, u32[]{:S(2)}) copy-start(f32[128,2048]{1,0:T(8,128)} %copy-done.4) | copy-start | bytes 3145732
  103.1 7.0 %collective-permute-start.9 = (f32[128,128]{1,0:T(8,128)S(1)}, f32[128,128]{1,0:T(8,128)}, u32[]{:S(2)}, u32[]{:S(2)}) collective-permute-start(f32[128,128]{1,0:T(8,128)S(1)} %add.8), channel_id=1, source_target_pairs={{0,2},{1,3},{2,0},{3,1},{4,6},{5,7},{6,4},{7,5},{8,10},{9,11},{10,... | collective-permute-start | bytes 196616 | tf_op jit(solution)/shard_map/ppermute | solution.py:414
  104.7 23.0 %all-to-all-start.3 = ((f32[32,32,128]{2,1,0:T(8,128)}), f32[32,32,128]{2,1,0:T(8,128)S(1)}, u32[]{:S(2)}, u32[]{:S(2)}) async-start(f32[32,32,128]{2,1,0:T(8,128)} %far_terms.1), calls=%async_computation.3 | async-start | bytes 1048576 | tf_op jit(solution)/shard_map/all_to_all | solution.py:410
  110.9 1.0 copy-start.14
  111.9 0.9 copy-start.17
